TPU v7x, 32 devices: a whole 2x2x4 slice. The times are simulated.
32 devices in a mesh: rows: 8 (over z, core), delay: 4 (over y, x).
Axes of the slice: x: 2, y: 2, z: 4, core: 2. Of those that a mesh axis runs over, the one named last changes fastest.
Arguments:
- retarded_tiles: bfloat16 [4, 512, 4, 128, 128], P('delay', 'rows'), may hold values from -0.125 to 0.125
- wanted_blocks: int32 [4, 8, 8, 16], P('delay', 'rows'), may hold values from 0 to 63, as said below
- tile_slots: int32 [4, 512, 4], P('delay', 'rows'), may hold values from 0 to 127, as said below
- diag_inverse: bfloat16 [512, 128, 128], P('rows')
- excitation: float32 [4, 512, 4, 128], P(None, 'rows'), may hold values from -6 to 6
- history_init: bfloat16 [4, 512, 4, 128], P('delay', 'rows'), may hold values from -6 to 6
Outputs:
- currents: float32 [4, 512, 4, 128], P(None, 'rows')
Inputs may be any that keep to these rules, and one draw needn't show every extreme that they name: `wanted_blocks`: for each bin, reader and owner, 16 distinct local block numbers of the owner. `tile_slots`: in each bin, every one of a reader's 8 * 16 taken blocks is the column block of at least one tile of the reader's row blocks.
All inputs are finite; a program needn't handle non-finite values.
Results may differ from a plain program's by a relative error of at most 0.0035.
Values may be sent and summed in bfloat16 or wider, within the bound.
A program may use at most 64 MiB of HBM per device.

v0:
```python
import jax
import jax.numpy as jnp
from jax import lax
from jax.sharding import PartitionSpec as P

STEPS = 4


def from_behind(array, axis, by):
    peers = lax.axis_size(axis)
    pairs = [(i, i + by) for i in range(peers) if 0 <= i + by < peers]
    return lax.ppermute(array, axis, pairs)


def body(retarded_tiles, wanted_blocks, tile_slots, diag_inverse, excitation, history_init):
    local_blocks = retarded_tiles.shape[1]
    listed = retarded_tiles.shape[2]
    requests = wanted_blocks[0, 0]
    slot_picks = tile_slots[0].reshape(-1)
    tile_block = retarded_tiles[0]
    position = lax.axis_index("delay")
    asked = lax.all_to_all(requests, "rows", split_axis=0, concat_axis=0, tiled=True)
    current = history_init[0]
    solved_list = []
    for moment in range(STEPS):
        looked_up = current[asked]
        arrived = lax.all_to_all(looked_up, "rows", split_axis=0, concat_axis=0, tiled=True)
        flat = arrived.reshape(-1, current.shape[1], current.shape[2])
        blocks = flat[slot_picks]
        blocks = blocks.reshape(local_blocks, listed, current.shape[1], current.shape[2])
        partial_value = jnp.einsum(
            "nleb,nlbc->nec", blocks, tile_block, preferred_element_type=jnp.float32
        )
        retarded = lax.psum(partial_value, "delay")
        driven = (excitation[moment] - retarded).astype(jnp.bfloat16)
        solved = jnp.einsum(
            "neb,nbc->nec", driven, diag_inverse, preferred_element_type=jnp.float32
        )
        solved_list.append(solved)
        if moment + 1 < STEPS:
            rounded = solved.astype(jnp.bfloat16)
            shifted = from_behind(current, "delay", 1)
            current = jnp.where(position == 0, rounded, shifted)
    return jnp.stack(solved_list)


def solution(mesh):
    return jax.shard_map(
        body,
        mesh=mesh,
        in_specs=(
            P("delay", "rows", None, None, None),
            P("delay", "rows", None, None),
            P("delay", "rows", None),
            P("rows", None, None),
            P(None, "rows", None, None),
            P("delay", "rows", None, None),
        ),
        out_specs=P(None, "rows", None, None),
        check_vma=False,
    )
```

profile of v0, /device:TPU:6, one launch (start us, length us, event | category | flops | bytes accessed | tf_op | source)
XLA Modules:
  0.0 265.3 jit_solution(13580528603090862192)
XLA Ops:
  6.5 5.0 %all-to-all-start = ((s32[8,1,16]{2,1,0:T(1,128)}), s32[8,1,16]{2,1,0:T(1,128)S(1)}, u32[]{:S(2)}, u32[]{:S(2)}) async-start(s32[8,1,16]{2,1,0:T(1,128)} %bitcast.115), calls=%async_computation | async-start | bytes 8192 | tf_op jit(solution)/shard_map/all_to_all | solution.py:22
  11.5 0.8 copy.9
  12.3 0.1 reshape_squeeze.3
  12.4 0.0 copy-start.2
  12.4 0.0 copy-start.1
  12.4 4.6 %all-to-all-done = s32[8,1,16]{2,1,0:T(1,128)S(1)} async-done(((s32[8,1,16]{2,1,0:T(1,128)}), s32[8,1,16]{2,1,0:T(1,128)S(1)}, u32[]{:S(2)}, u32[]{:S(2)}) %all-to-all-start) | async-done | bytes 544 | tf_op jit(solution)/shard_map/all_to_all | solution.py:22
  17.0 0.1 reshape.93
  17.1 2.2 gather_fusion
  19.4 3.4 %all-to-all-start.1 = ((bf16[8,16,4,128]{3,2,1,0:T(4,128)(2,1)}), bf16[8,16,4,128]{3,2,1,0:T(4,128)(2,1)S(1)}, u32[]{:S(2)}, u32[]{:S(2)}) async-start(bf16[8,16,4,128]{3,2,1,0:T(4,128)(2,1)} %bitcast.5), calls=%async_computation.1 | async-start | bytes 262144 | tf_op jit(solution)/shard_map/all_to_all | solution.py:27
  22.7 0.0 all-reduce.5.cloned.1.call-start
  22.8 6.6 %all-to-all-done.1 = bf16[8,16,4,128]{3,2,1,0:T(4,128)(2,1)S(1)} async-done(((bf16[8,16,4,128]{3,2,1,0:T(4,128)(2,1)}), bf16[8,16,4,128]{3,2,1,0:T(4,128)(2,1)S(1)}, u32[]{:S(2)}, u32[]{:S(2)}) %all-to-all-start.1) | async-done | bytes 131104 | tf_op jit(solution)/shard_map/all_to_all | solution.py:27
  29.5 1.0 gather_fusion.1
  30.4 5.3 %fusion.8 = f32[64,4,128]{2,1,0:T(4,128)} fusion(bf16[64,4,4,128]{3,2,1,0:T(4,128)(2,1)S(1)} %bitcast.91, bf16[1,64,4,128,128]{4,3,2,1,0:T(8,128)(2,1)} %param.6), kind=kOutput, calls=%fused_computation.16 | convolution fusion | flops 33554432 | bytes 8781824 | tf_op jit(solution)/shard_map/nleb,nlbc->nec/dot_general | solution.py:31
  35.8 0.0 all-reduce.5.cloned.1.call-update
  35.8 0.0 all-reduce.7.cloned.1.call-start
  35.9 0.0 copy-done.2
  35.9 1.3 collective-permute-start
  37.2 5.6 %collective-permute-done = bf16[64,4,128]{2,1,0:T(4,128)(2,1)S(1)} collective-permute-done((bf16[64,4,128]{2,1,0:T(4,128)(2,1)S(1)}, bf16[64,4,128]{2,1,0:T(4,128)(2,1)S(1)}, u32[]{:S(2)}, u32[]{:S(2)}) %collective-permute-start) | collective-permute-done | bytes 65568 | tf_op jit(solution)/shard_map/ppermute | solution.py:12
  42.7 33.3 %all-reduce.5.cloned.1.call-done = f32[64,4,128]{2,1,0:T(4,128)} async-done(((f32[64,4,128]{2,1,0:T(4,128)}), f32[64,4,128]{2,1,0:T(4,128)}) %all-reduce.5.cloned.1.call-update) | async-done | bytes 131088 | tf_op jit(solution)/shard_map/psum | solution.py:34
  76.0 1.6 convert_select_fusion.2
  77.6 0.8 gather_fusion.2
  78.3 11.2 %all_to_all.32 = bf16[8,16,4,128]{3,2,1,0:T(4,128)(2,1)S(1)} all-to-all(bf16[8,16,4,128]{3,2,1,0:T(4,128)(2,1)S(1)} %bitcast.106), channel_id=1, replica_groups=mesh['rows'=8,'delay'=4] {'rows'}, dimensions={0} | all-to-all | bytes 262144 | tf_op jit(solution)/shard_map/all_to_all | solution.py:27
  89.5 1.0 gather_fusion.3
  90.5 5.3 %fusion.11 = f32[64,4,128]{2,1,0:T(4,128)} fusion(bf16[64,4,4,128]{3,2,1,0:T(4,128)(2,1)S(1)} %bitcast.92, bf16[1,64,4,128,128]{4,3,2,1,0:T(8,128)(2,1)} %param.6), kind=kOutput, calls=%fused_computation.17 | convolution fusion | flops 33554432 | bytes 8781824 | tf_op jit(solution)/shard_map/nleb,nlbc->nec/dot_general | solution.py:31
  95.8 0.0 all-reduce.7.cloned.1.call-update
  95.8 0.0 all-reduce.9.cloned.1.call-start
  95.9 1.3 collective-permute-start.1
  97.2 38.9 %all-reduce.7.cloned.1.call-done = f32[64,4,128]{2,1,0:T(4,128)} async-done(((f32[64,4,128]{2,1,0:T(4,128)}), f32[64,4,128]{2,1,0:T(4,128)}) %all-reduce.7.cloned.1.call-update) | async-done | bytes 131088 | tf_op jit(solution)/shard_map/psum | solution.py:34
  136.1 1.5 fusion.26
  137.6 0.0 collective-permute-done.1
  137.7 0.7 gather_fusion.4
  138.4 11.2 %all_to_all.33 = bf16[8,16,4,128]{3,2,1,0:T(4,128)(2,1)S(1)} all-to-all(bf16[8,16,4,128]{3,2,1,0:T(4,128)(2,1)S(1)} %bitcast.107), channel_id=1, replica_groups=mesh['rows'=8,'delay'=4] {'rows'}, dimensions={0} | all-to-all | bytes 262144 | tf_op jit(solution)/shard_map/all_to_all | solution.py:27
  149.6 1.0 gather_fusion.5
  150.6 5.3 %fusion.14 = f32[64,4,128]{2,1,0:T(4,128)} fusion(bf16[64,4,4,128]{3,2,1,0:T(4,128)(2,1)S(1)} %bitcast.93, bf16[1,64,4,128,128]{4,3,2,1,0:T(8,128)(2,1)} %param.6), kind=kOutput, calls=%fused_computation.18 | convolution fusion | flops 33554432 | bytes 8781824 | tf_op jit(solution)/shard_map/nleb,nlbc->nec/dot_general | solution.py:31
  155.9 0.0 all-reduce.9.cloned.1.call-update
  155.9 0.0 all-reduce.11.cloned.1.call-start
  156.0 1.3 collective-permute-start.2
  157.3 38.9 %all-reduce.9.cloned.1.call-done = f32[64,4,128]{2,1,0:T(4,128)} async-done(((f32[64,4,128]{2,1,0:T(4,128)}), f32[64,4,128]{2,1,0:T(4,128)}) %all-reduce.9.cloned.1.call-update) | async-done | bytes 131088 | tf_op jit(solution)/shard_map/psum | solution.py:34
  196.2 1.5 fusion.28
  197.7 0.0 collective-permute-done.2
  197.7 0.7 gather_fusion.6
  198.5 11.2 %all_to_all.34 = bf16[8,16,4,128]{3,2,1,0:T(4,128)(2,1)S(1)} all-to-all(bf16[8,16,4,128]{3,2,1,0:T(4,128)(2,1)S(1)} %bitcast.105), channel_id=1, replica_groups=mesh['rows'=8,'delay'=4] {'rows'}, dimensions={0} | all-to-all | bytes 262144 | tf_op jit(solution)/shard_map/all_to_all | solution.py:27
  209.7 1.0 gather_fusion.7
  210.7 5.3 %fusion.17 = f32[64,4,128]{2,1,0:T(4,128)} fusion(bf16[64,4,4,128]{3,2,1,0:T(4,128)(2,1)S(1)} %bitcast.90, bf16[1,64,4,128,128]{4,3,2,1,0:T(8,128)(2,1)} %param.6), kind=kOutput, calls=%fused_computation.19 | convolution fusion | flops 33554432 | bytes 8781824 | tf_op jit(solution)/shard_map/nleb,nlbc->nec/dot_general | solution.py:31
  216.0 0.0 all-reduce.11.cloned.1.call-update
  216.0 40.2 %all-reduce.11.cloned.1.call-done = f32[64,4,128]{2,1,0:T(4,128)} async-done(((f32[64,4,128]{2,1,0:T(4,128)}), f32[64,4,128]{2,1,0:T(4,128)}) %all-reduce.11.cloned.1.call-update) | async-done | bytes 131088 | tf_op jit(solution)/shard_map/psum | solution.py:34
  256.3 1.5 convolution_bitcast_fusion
  257.8 0.9 pad_maximum_fusion
  (9 shorter events, 0.1 us)
Async XLA Ops:
  6.5 69.5 %copy-start = (bf16[64,128,128]{2,1,0:T(8,128)(2,1)S(1)}, bf16[64,128,128]{2,1,0:T(8,128)(2,1)}, u32[]{:S(2)}) copy-start(bf16[64,128,128]{2,1,0:T(8,128)(2,1)} %param.9) | copy-start | bytes 6291460
  6.5 10.5 %all-to-all-start = ((s32[8,1,16]{2,1,0:T(1,128)}), s32[8,1,16]{2,1,0:T(1,128)S(1)}, u32[]{:S(2)}, u32[]{:S(2)}) async-start(s32[8,1,16]{2,1,0:T(1,128)} %bitcast.115), calls=%async_computation | async-start | bytes 8192 | tf_op jit(solution)/shard_map/all_to_all | solution.py:22
  12.4 23.4 %copy-start.2 = (bf16[1,64,4,128]{3,2,1,0:T(4,128)(2,1)S(1)}, bf16[1,64,4,128]{3,2,1,0:T(4,128)(2,1)}, u32[]{:S(2)}) copy-start(bf16[1,64,4,128]{3,2,1,0:T(4,128)(2,1)} %param.11) | copy-start | bytes 196612
  12.4 63.6 %copy-start.1 = (f32[4,64,4,128]{3,2,1,0:T(4,128)S(1)}, f32[4,64,4,128]{3,2,1,0:T(4,128)}, u32[]{:S(2)}) copy-start(f32[4,64,4,128]{3,2,1,0:T(4,128)} %param.10) | copy-start | bytes 1572868
  19.4 10.1 %all-to-all-start.1 = ((bf16[8,16,4,128]{3,2,1,0:T(4,128)(2,1)}), bf16[8,16,4,128]{3,2,1,0:T(4,128)(2,1)S(1)}, u32[]{:S(2)}, u32[]{:S(2)}) async-start(bf16[8,16,4,128]{3,2,1,0:T(4,128)(2,1)} %bitcast.5), calls=%async_computation.1 | async-start | bytes 262144 | tf_op jit(solution)/shard_map/all_to_all | solution.py:27
  22.7 53.3 %all-reduce.5.cloned.1.call-start = ((), (), s32[]{:S(2)}) async-start(), calls=%async_computation.5 | async-start | bytes 262144 | tf_op jit(solution)/shard_map/psum | solution.py:34
  35.8 100.3 %all-reduce.7.cloned.1.call-start = ((), (), s32[]{:S(2)}) async-start(), calls=%async_computation.6 | async-start | bytes 262144 | tf_op jit(solution)/shard_map/psum | solution.py:34
  35.9 6.9 %collective-permute-start = (bf16[64,4,128]{2,1,0:T(4,128)(2,1)S(1)}, bf16[64,4,128]{2,1,0:T(4,128)(2,1)S(1)}, u32[]{:S(2)}, u32[]{:S(2)}) collective-permute-start(bf16[64,4,128]{2,1,0:T(4,128)(2,1)S(1)} %bitcast.110), channel_id=1, source_target_pairs={{0,1},{1,2},{2,3},{4,5},{5,6},{6,7},{8,9},{9,10},{10,11},{12,13},{... | collective-permute-start | bytes 196616 | tf_op jit(solution)/shard_map/ppermute | solution.py:12
  95.8 100.3 %all-reduce.9.cloned.1.call-start = ((), (), s32[]{:S(2)}) async-start(), calls=%async_computation.7 | async-start | bytes 262144 | tf_op jit(solution)/shard_map/psum | solution.py:34
  95.9 41.7 %collective-permute-start.1 = (bf16[64,4,128]{2,1,0:T(4,128)(2,1)S(1)}, bf16[64,4,128]{2,1,0:T(4,128)(2,1)S(1)}, u32[]{:S(2)}, u32[]{:S(2)}) collective-permute-start(bf16[64,4,128]{2,1,0:T(4,128)(2,1)S(1)} %get-tuple-element.5), channel_id=1, source_target_pairs={{0,1},{1,2},{2,3},{4,5},{5,6},{6,7},{8,9},{9,10},{10,11},{12,13},{... | collective-permute-start | bytes 196616 | tf_op jit(solution)/shard_map/ppermute | solution.py:12
  155.9 100.3 %all-reduce.11.cloned.1.call-start = ((), (), s32[]{:S(2)}) async-start(), calls=%async_computation.8 | async-start | bytes 262144 | tf_op jit(solution)/shard_map/psum | solution.py:34
  156.0 41.7 %collective-permute-start.2 = (bf16[64,4,128]{2,1,0:T(4,128)(2,1)S(1)}, bf16[64,4,128]{2,1,0:T(4,128)(2,1)S(1)}, u32[]{:S(2)}, u32[]{:S(2)}) collective-permute-start(bf16[64,4,128]{2,1,0:T(4,128)(2,1)S(1)} %bitcast.103), channel_id=1, source_target_pairs={{0,1},{1,2},{2,3},{4,5},{5,6},{6,7},{8,9},{9,10},{10,11},{12,13},{... | collective-permute-start | bytes 196616 | tf_op jit(solution)/shard_map/ppermute | solution.py:12
Sparse Core Ops, SparseCore 0:
  35.9 40.0 all-reduce.4
  96.0 40.0 all-reduce.6
  156.1 40.0 all-reduce.8
  216.1 40.0 all-reduce.10
where the time goes:
time: 268 us; the launch traced here: 265 us
  waiting for transfers between devices  168 us (63%)
  blocking collectives  33.5 us (12%)
  matrix products  27.5 us (10%)
  between operations  13.3 us (5%)
  starting transfers between devices  12.4 us (5%)
  local copies, waits for them, and re-layouts  9.37 us (3%)
    psum x4, waiting for transfers between devices, body(): retarded = lax.psum(partial_value, 'delay')  151 us
    all_to_all x3, blocking collectives, body(): lax.all_to_all(looked_up, 'rows', split_axis=0, concat_axis=0, tiled=True)  33.5 us
    dot_general x4, matrix products, body(): jnp.einsum('nleb,nlbc->nec', blocks, tile_block, preferred_element_type=j...  21.3 us
    all_to_all x1, waiting for transfers between devices, body(): lax.all_to_all(looked_up, 'rows', split_axis=0, concat_axis=0, tiled=True)  6.64 us
    dot_general x4, matrix products, body(): jnp.einsum('neb,nbc->nec', driven, diag_inverse, preferred_element_type=j...  6.18 us
    ppermute x3, waiting for transfers between devices, from_behind(): return lax.ppermute(array, axis, pairs)  5.56 us
  transfers between devices with their start and end apart: 9, of which 7 were waited for; matrix products, arithmetic and copies ran while one was open for 1% of the time, Pallas kernels for 0%

commit v1 on v0

v1 whole, which is shorter than its diff:
```python
import functools

import jax
import jax.numpy as jnp
from jax import lax
from jax.experimental import pallas as pl
from jax.experimental.pallas import tpu as pltpu
from jax.sharding import PartitionSpec as P

MESH = pl.DeviceIdType.MESH
F32 = jnp.float32
BF16 = jnp.bfloat16


def row_of(shape):
    return lax.broadcasted_iota(jnp.int32, shape, 0)


def lane_of(shape):
    return lax.broadcasted_iota(jnp.int32, shape, 1)


def dot(a, b):
    return jnp.dot(a, b, preferred_element_type=F32)


def kernel(
    sizes,
    history, wanted, slots, tiles_hbm, diag_hbm, excitation_hbm,
    out,
    tiles, diag, excitation, picks, spots, ask_out, ask_in, source, sent, got, lhs,
    part_out, part_in, driven,
    load_sem, ask_send, ask_recv, shift_send, shift_recv, swap_send, swap_recv,
    part_send, part_recv, driven_send, driven_recv,
):
    readers, bins, steps, n, listed, exc, cap, width = sizes
    me = lax.axis_index("rows")
    bin_at = lax.axis_index("delay")
    rows = n * exc
    chunk = cap * exc
    group = 16 // exc
    groups = rows // 16

    loads = [
        pltpu.make_async_copy(excitation_hbm, excitation, load_sem.at[0]),
        pltpu.make_async_copy(tiles_hbm, tiles, load_sem.at[1]),
        pltpu.make_async_copy(diag_hbm, diag, load_sem.at[2]),
    ]
    for load in loads:
        load.start()

    barrier = pltpu.get_barrier_semaphore()
    for d in range(1, readers):
        pl.semaphore_signal(barrier, inc=1, device_id={"rows": lax.rem(me + d, readers)}, device_id_type=MESH)
    for d in range(1, bins):
        pl.semaphore_signal(barrier, inc=1, device_id={"delay": lax.rem(bin_at + d, bins)}, device_id_type=MESH)

    total = readers * cap
    shape = (total, readers)
    spread = jnp.where(lax.div(row_of(shape), cap) == lane_of(shape), 1.0, 0.0).astype(F32)
    every = dot(spread, wanted[...].astype(F32))
    shape = (total, cap)
    own = jnp.where(lax.rem(row_of(shape), cap) == lane_of(shape), every, 0.0)
    ask_out[...] = jnp.broadcast_to(jnp.sum(own, axis=1, keepdims=True), (total, width))

    pl.semaphore_wait(barrier, readers - 1 + bins - 1)

    def ask(d):
        peer = lax.rem(me + d, readers)
        return pltpu.make_async_remote_copy(
            src_ref=ask_out.at[pl.ds(pl.multiple_of(peer * cap, cap), cap)],
            dst_ref=ask_in.at[pl.ds(pl.multiple_of(me * cap, cap), cap)],
            send_sem=ask_send.at[d], recv_sem=ask_recv.at[d],
            device_id={"rows": peer}, device_id_type=MESH,
        )

    def asked(d):
        peer = lax.rem(me + readers - d, readers)
        there = ask_in.at[pl.ds(pl.multiple_of(peer * cap, cap), cap)]
        return pltpu.make_async_remote_copy(
            src_ref=there, dst_ref=there,
            send_sem=ask_send.at[d], recv_sem=ask_recv.at[d],
            device_id={"rows": peer}, device_id_type=MESH,
        )

    for d in range(1, readers):
        ask(d).start()

    def shift(s):
        return pltpu.make_async_remote_copy(
            src_ref=history, dst_ref=source.at[s],
            send_sem=shift_send.at[s], recv_sem=shift_recv.at[s],
            device_id={"delay": lax.rem(bin_at + s, bins)}, device_id_type=MESH,
        )

    for s in range(1, min(steps, bins)):
        @pl.when(bin_at + s < bins)
        def _():
            shift(s).start()

    mine = pl.ds(pl.multiple_of(me * cap, cap), cap)
    ask_in[mine] = ask_out[mine]
    source[0] = history[...]

    here = lax.div(row_of((rows, n)), exc) == lane_of((rows, n))
    listing = slots[...].astype(F32)
    shape = (rows, total * exc)
    lanes = lane_of(shape).astype(F32)
    which = lax.rem(row_of((rows, 1)), exc).astype(F32)
    for l in range(listed):
        slot = jnp.sum(jnp.where(here, listing[l : l + 1], 0.0), axis=1, keepdims=True)
        target = slot * exc + which
        spots[l] = jnp.where(lanes == target, 1.0, 0.0).astype(BF16)

    for d in range(1, readers):
        asked(d).wait_recv()
    shape = (total * exc, total)
    spread = jnp.where(lax.div(row_of(shape), exc) == lane_of(shape), 1.0, 0.0).astype(F32)
    target = dot(spread, ask_in[...])
    shape = (total * exc, width)
    target = target * exc + lax.rem(row_of(shape), exc).astype(F32)
    for h in range(rows // width):
        lanes = (lane_of(shape) + h * width).astype(F32)
        picks[:, h * width : (h + 1) * width] = jnp.where(lanes == target, 1.0, 0.0).astype(BF16)

    def chosen(products):
        place = lax.div(row_of((16, width)), exc)
        kept = products[:, :width]
        for i in range(1, group):
            kept = jnp.where(place == i, products[:, i * width : (i + 1) * width], kept)
        return kept

    def swap(t, d):
        peer = lax.rem(me + d, readers)
        return pltpu.make_async_remote_copy(
            src_ref=sent.at[t, pl.ds(pl.multiple_of(peer * chunk, chunk), chunk)],
            dst_ref=got.at[t, pl.ds(pl.multiple_of(me * chunk, chunk), chunk)],
            send_sem=swap_send.at[t, d], recv_sem=swap_recv.at[t, d],
            device_id={"rows": peer}, device_id_type=MESH,
        )

    def swapped(t, d):
        peer = lax.rem(me + readers - d, readers)
        there = got.at[t, pl.ds(pl.multiple_of(peer * chunk, chunk), chunk)]
        return pltpu.make_async_remote_copy(
            src_ref=there, dst_ref=there,
            send_sem=swap_send.at[t, d], recv_sem=swap_recv.at[t, d],
            device_id={"rows": peer}, device_id_type=MESH,
        )

    def part(t, k):
        return pltpu.make_async_remote_copy(
            src_ref=part_out.at[t], dst_ref=part_in.at[t, k],
            send_sem=part_send.at[t], recv_sem=part_recv.at[t, k],
            device_id={"delay": 0}, device_id_type=MESH,
        )

    def tell(t, d):
        return pltpu.make_async_remote_copy(
            src_ref=driven.at[t], dst_ref=driven.at[t],
            send_sem=driven_send.at[t, d], recv_sem=driven_recv.at[t],
            device_id={"delay": d}, device_id_type=MESH,
        )

    def solve(u):
        later = u + 1 + bin_at

        def some(q, c):
            for i in range(4):
                g = q * 4 + i
                at = pl.ds(pl.multiple_of(g * 16, 16), 16)
                right = jnp.concatenate([diag[g * group + j] for j in range(group)], axis=1)
                value = chosen(dot(driven[u, at], right))
                out[u, at] = value

                @pl.when(later < steps)
                def _():
                    source[jnp.minimum(later, steps - 1), at] = value.astype(BF16)
            return c

        lax.fori_loop(0, groups // 4, some, 0)

    def step(t, carry):
        @pl.when((t > 0) & (bin_at >= t))
        def _():
            pltpu.make_async_remote_copy(
                src_ref=history, dst_ref=source.at[t],
                send_sem=shift_send.at[t], recv_sem=shift_recv.at[t],
                device_id={"delay": lax.rem(bin_at + 1, bins)}, device_id_type=MESH,
            ).wait_recv()

        @pl.when((bin_at > 0) & (bin_at < t))
        def _():
            u = t - 1 - bin_at
            tell(u, 0).wait_recv()

            @pl.when(u == 0)
            def _():
                loads[2].wait()

            solve(u)

        sent[t] = dot(picks[...], source[t]).astype(BF16)
        for d in range(1, readers):
            swap(t, d).start()
        mine = pl.ds(pl.multiple_of(me * chunk, chunk), chunk)
        got[t, mine] = sent[t, mine]
        for d in range(1, readers):
            swapped(t, d).wait_recv()
        arrived = got[t]
        for l in range(listed):
            lhs[:, l * width : (l + 1) * width] = dot(spots[l], arrived).astype(BF16)

        @pl.when(t == 0)
        def _():
            loads[0].wait()
            loads[1].wait()

        def some(q, c):
            for i in range(4):
                g = q * 4 + i
                at = pl.ds(pl.multiple_of(g * 16, 16), 16)
                right = jnp.concatenate([tiles[g * group + j] for j in range(group)], axis=1)
                part_out[t, at] = chosen(dot(lhs[at], right))
            return c

        lax.fori_loop(0, groups // 4, some, 0)

        @pl.when(bin_at > 0)
        def _():
            part(t, bin_at).start()

        @pl.when(bin_at == 0)
        def _():
            value = part_out[t]
            for k in range(1, bins):
                part(t, k).wait_recv()
                value = value + part_in[t, k]
            driven[t] = (excitation[t] - value).astype(BF16)
            for d in range(1, bins):
                tell(t, d).start()

            @pl.when(t == 0)
            def _():
                loads[2].wait()

            solve(t)

        return carry

    lax.fori_loop(0, steps, step, 0)

    @pl.when(bin_at > 0)
    def _():
        def last(u, c):
            @pl.when(u >= steps - 1 - bin_at)
            def _():
                tell(u, 0).wait_recv()

                @pl.when(u == 0)
                def _():
                    loads[2].wait()

                solve(u)
            return c

        lax.fori_loop(0, steps, last, 0)

    for d in range(1, readers):
        ask(d).wait_send()
    for s in range(1, min(steps, bins)):
        @pl.when(bin_at + s < bins)
        def _():
            shift(s).wait_send()

    def drain(t, c):
        for d in range(1, readers):
            swap(t, d).wait_send()

        @pl.when(bin_at > 0)
        def _():
            part(t, bin_at).wait_send()

        @pl.when(bin_at == 0)
        def _():
            for d in range(1, bins):
                tell(t, d).wait_send()
        return c

    lax.fori_loop(0, steps, drain, 0)


def body(retarded_tiles, wanted_blocks, tile_slots, diag_inverse, excitation, history_init):
    readers, bins = lax.axis_size("rows"), lax.axis_size("delay")
    _, n, listed, width, _ = retarded_tiles.shape
    steps, _, exc, _ = excitation.shape
    cap = wanted_blocks.shape[-1]
    rows, taken = n * exc, readers * cap * exc
    sizes = (readers, bins, steps, n, listed, exc, cap, width)
    vmem = pl.BlockSpec(memory_space=pltpu.VMEM)
    anywhere = pl.BlockSpec(memory_space=pl.ANY)
    dma = pltpu.SemaphoreType.DMA
    solved = pl.pallas_call(
        functools.partial(kernel, sizes),
        out_shape=jax.ShapeDtypeStruct((steps, rows, width), F32),
        in_specs=[vmem, vmem, vmem, anywhere, anywhere, anywhere],
        out_specs=vmem,
        scratch_shapes=[
            pltpu.VMEM((n, listed * width, width), BF16),
            pltpu.VMEM((n, width, width), BF16),
            pltpu.VMEM((steps, rows, width), F32),
            pltpu.VMEM((taken, rows), BF16),
            pltpu.VMEM((listed, rows, taken), BF16),
            pltpu.VMEM((readers * cap, width), F32),
            pltpu.VMEM((readers * cap, width), F32),
            pltpu.VMEM((steps, rows, width), BF16),
            pltpu.VMEM((steps, taken, width), BF16),
            pltpu.VMEM((steps, taken, width), BF16),
            pltpu.VMEM((rows, listed * width), BF16),
            pltpu.VMEM((steps, rows, width), F32),
            pltpu.VMEM((steps, bins, rows, width), F32),
            pltpu.VMEM((steps, rows, width), BF16),
            dma((3,)),
            dma((readers,)),
            dma((readers,)),
            dma((steps,)),
            dma((steps,)),
            dma((steps, readers)),
            dma((steps, readers)),
            dma((steps,)),
            dma((steps, bins)),
            dma((steps, bins)),
            dma((steps,)),
        ],
        compiler_params=pltpu.CompilerParams(
            collective_id=0, has_side_effects=True, vmem_limit_bytes=57 << 20
        ),
        cost_estimate=pl.CostEstimate(
            flops=2 * steps * rows * width * width * (listed + 1), transcendentals=0,
            bytes_accessed=2 * n * width * width * (listed + 1),
        ),
    )(
        history_init.reshape(rows, width),
        wanted_blocks.reshape(readers, cap),
        tile_slots.reshape(n, listed).T,
        retarded_tiles.reshape(n, listed * width, width),
        diag_inverse,
        excitation.reshape(steps, rows, width),
    )
    return solved.reshape(steps, n, exc, width)


def solution(mesh):
    return jax.shard_map(
        body,
        mesh=mesh,
        in_specs=(
            P("delay", "rows", None, None, None),
            P("delay", "rows", None, None),
            P("delay", "rows", None),
            P("rows", None, None),
            P(None, "rows", None, None),
            P("delay", "rows", None, None),
        ),
        out_specs=P(None, "rows", None, None),
        check_vma=False,
    )
```

time: 268 us -> 60.3 us (0.22)
  waiting for transfers between devices: 168 us -> 0 us
  Pallas kernels: 0 us -> 58.2 us
  blocking collectives: 33.5 us -> 0 us
  matrix products: 27.5 us -> 0 us
  between operations: 13.3 us -> 0.01 us
  starting transfers between devices: 12.4 us -> 0 us
  local copies, waits for them, and re-layouts: 9.37 us -> 1.87 us
    psum x4 -> x0, waiting for transfers between devices: 151 us -> none  [body(): retarded = lax.psum(partial_value, 'delay')]
    pallas_call x0 -> x1, Pallas kernels: none -> 58.2 us  [body(): pl.pallas_call(functools.partial(kernel, sizes), out_shape=jax.ShapeDtype...]
    all_to_all x3 -> x0, blocking collectives: 33.5 us -> none  [body(): lax.all_to_all(looked_up, 'rows', split_axis=0, concat_axis=0, tiled=True)]
    dot_general x8 -> x0, matrix products: 27.5 us -> none  [the longest x4 21.3 us: body(): jnp.einsum('nleb,nlbc->nec', blocks, tile_block, preferred_element_type=j...]
    all_to_all x2 -> x0, waiting for transfers between devices: 11.2 us -> none  [the longest x1 6.64 us: body(): lax.all_to_all(looked_up, 'rows', split_axis=0, concat_axis=0, tiled=True)]
    gather x8 -> x0, local copies, waits for them, and re-layouts: 8.4 us -> none  [the longest x4 4.48 us: body(): looked_up = current[asked]]
    all_to_all x2 -> x0, starting transfers between devices: 8.38 us -> none  [the longest x1 5.01 us: body(): lax.all_to_all(requests, 'rows', split_axis=0, concat_axis=0, tiled=True)]
    ppermute x3 -> x0, waiting for transfers between devices: 5.56 us -> none  [from_behind(): return lax.ppermute(array, axis, pairs)]
  transfers between devices with their start and end apart: 9 -> 0, of which waited for: 7 -> 0; matrix products, arithmetic and copies ran while one was open for 1% -> 0% of each run, Pallas kernels for 0% -> 0%
where the time goes in v1:
time: 60.3 us; the launch traced here: 60.1 us
  Pallas kernels  58.2 us (97%)
  local copies, waits for them, and re-layouts  1.87 us (3%)
    pallas_call x1, Pallas kernels, body(): pl.pallas_call(functools.partial(kernel, sizes), out_shape=jax.ShapeDtype...  58.2 us
    unnamed x1, local copies, waits for them, and re-layouts  1.87 us

profile of v1, /device:TPU:6, one launch (start us, length us, event | category | flops | bytes accessed | tf_op | source)
XLA Modules:
  0.0 60.1 jit_solution(7344068757983026200)
XLA Ops:
  0.0 58.2 %shard_map.64 = f32[4,256,128]{2,1,0:T(8,128)} custom-call(bf16[256,128]{1,0:T(8,128)(2,1)} %bitcast.11, s32[8,16]{1,0:T(8,128)} %bitcast.12, s32[4,64]{1,0:T(4,128)} %bitcast.13, bf16[64,512,128]{2,1,0:T(8,128)(2,1)} %bitcast.8, bf16[64,128,128]{2,1,0:T(8,128)(2,1)} %diag_hbm.1, f32[4,256,128]{2,1,0:T(8,128)} %bitcast.10), custom_call_target="tpu_custom_call" | custom-call | flops 167772160 | bytes 10485760 | tf_op jit(solution)/shard_map/pallas_call | solution.py:303
  58.2 1.9 %copy.8 = f32[4,64,4,128]{3,2,1,0:T(4,128)} copy(f32[4,64,4,128]{3,2,1,0:T(4,128)} %bitcast.9) | data formatting | bytes 1048576

commit v2 on v1

--- a/solution.py
+++ b/solution.py
@@ -29,7 +29,7 @@
     history, wanted, slots, tiles_hbm, diag_hbm, excitation_hbm,
     out,
     tiles, diag, excitation, picks, spots, ask_out, ask_in, source, sent, got, lhs,
-    part_out, part_in, driven,
+    part_own, part_out, part_in, driven,
     load_sem, ask_send, ask_recv, shift_send, shift_recv, swap_send, swap_recv,
     part_send, part_recv, driven_send, driven_recv,
 ):
@@ -163,7 +163,7 @@
         )
 
     def solve(u):
-        later = u + 1 + bin_at
+        later = jnp.minimum(u + 1 + bin_at, steps)
 
         def some(q, c):
             for i in range(4):
@@ -172,10 +172,7 @@
                 right = jnp.concatenate([diag[g * group + j] for j in range(group)], axis=1)
                 value = chosen(dot(driven[u, at], right))
                 out[u, at] = value
-
-                @pl.when(later < steps)
-                def _():
-                    source[jnp.minimum(later, steps - 1), at] = value.astype(BF16)
+                source[later, at] = value.astype(BF16)
             return c
 
         lax.fori_loop(0, groups // 4, some, 0)
@@ -221,7 +218,9 @@
                 g = q * 4 + i
                 at = pl.ds(pl.multiple_of(g * 16, 16), 16)
                 right = jnp.concatenate([tiles[g * group + j] for j in range(group)], axis=1)
-                part_out[t, at] = chosen(dot(lhs[at], right))
+                value = chosen(dot(lhs[at], right))
+                part_out[t, at] = value.astype(BF16)
+                part_own[at] = value
             return c
 
         lax.fori_loop(0, groups // 4, some, 0)
@@ -232,10 +231,10 @@
 
         @pl.when(bin_at == 0)
         def _():
-            value = part_out[t]
+            value = part_own[...]
             for k in range(1, bins):
                 part(t, k).wait_recv()
-                value = value + part_in[t, k]
+                value = value + part_in[t, k].astype(F32)
             driven[t] = (excitation[t] - value).astype(BF16)
             for d in range(1, bins):
                 tell(t, d).start()
@@ -298,7 +297,7 @@
     rows, taken = n * exc, readers * cap * exc
     sizes = (readers, bins, steps, n, listed, exc, cap, width)
     vmem = pl.BlockSpec(memory_space=pltpu.VMEM)
-    anywhere = pl.BlockSpec(memory_space=pl.ANY)
+    anywhere = pl.BlockSpec(memory_space=pltpu.HBM)
     dma = pltpu.SemaphoreType.DMA
     solved = pl.pallas_call(
         functools.partial(kernel, sizes),
@@ -313,12 +312,13 @@
             pltpu.VMEM((listed, rows, taken), BF16),
             pltpu.VMEM((readers * cap, width), F32),
             pltpu.VMEM((readers * cap, width), F32),
-            pltpu.VMEM((steps, rows, width), BF16),
+            pltpu.VMEM((steps + 1, rows, width), BF16),
             pltpu.VMEM((steps, taken, width), BF16),
             pltpu.VMEM((steps, taken, width), BF16),
             pltpu.VMEM((rows, listed * width), BF16),
-            pltpu.VMEM((steps, rows, width), F32),
-            pltpu.VMEM((steps, bins, rows, width), F32),
+            pltpu.VMEM((rows, width), F32),
+            pltpu.VMEM((steps, rows, width), BF16),
+            pltpu.VMEM((steps, bins, rows, width), BF16),
             pltpu.VMEM((steps, rows, width), BF16),
             dma((3,)),
             dma((readers,)),
@@ -333,7 +333,7 @@
             dma((steps,)),
         ],
         compiler_params=pltpu.CompilerParams(
-            collective_id=0, has_side_effects=True, vmem_limit_bytes=57 << 20
+            collective_id=0, has_side_effects=True, vmem_limit_bytes=44 << 20
         ),
         cost_estimate=pl.CostEstimate(
             flops=2 * steps * rows * width * width * (listed + 1), transcendentals=0,

time: 60.3 us -> 54.3 us (0.900)
  Pallas kernels: 58.2 us -> 48.4 us
  local copies, waits for them, and re-layouts: 1.87 us -> 5.63 us
    pallas_call x1, Pallas kernels: 58.2 us -> 48.4 us  [body(): pl.pallas_call(functools.partial(kernel, sizes), out_shape=jax.ShapeDtype...]
    unnamed x1 -> x11, local copies, waits for them, and re-layouts: 1.87 us -> 5.63 us
where the time goes in v2:
time: 54.3 us; the launch traced here: 54 us
  Pallas kernels  48.4 us (89%)
  local copies, waits for them, and re-layouts  5.63 us (10%)
    pallas_call x1, Pallas kernels, body(): pl.pallas_call(functools.partial(kernel, sizes), out_shape=jax.ShapeDtype...  48.4 us
    unnamed x11, local copies, waits for them, and re-layouts  5.63 us

profile of v2, /device:TPU:6, one launch (start us, length us, event | category | flops | bytes accessed | tf_op | source)
XLA Modules:
  0.0 54.0 jit_solution(10951833599491448432)
XLA Ops:
  0.0 0.0 copy-start
  0.0 1.6 %copy-done = bf16[64,128,128]{2,1,0:T(8,128)(2,1)S(1)} copy-done((bf16[64,128,128]{2,1,0:T(8,128)(2,1)S(1)}, bf16[64,128,128]{2,1,0:T(8,128)(2,1)}, u32[]{:S(2)}) %copy-start) | copy-done | bytes 2097176
  1.6 0.0 copy-start.1
  1.6 1.0 %copy-done.1 = f32[4,64,4,128]{3,2,1,0:T(4,128)S(1)} copy-done((f32[4,64,4,128]{3,2,1,0:T(4,128)S(1)}, f32[4,64,4,128]{3,2,1,0:T(4,128)}, u32[]{:S(2)}) %copy-start.1) | copy-done | bytes 524312
  2.6 0.0 copy-start.2
  2.6 0.8 %copy-done.2 = bf16[1,64,4,128]{3,2,1,0:T(4,128)(2,1)S(1)} copy-done((bf16[1,64,4,128]{3,2,1,0:T(4,128)(2,1)S(1)}, bf16[1,64,4,128]{3,2,1,0:T(4,128)(2,1)}, u32[]{:S(2)}) %copy-start.2) | copy-done | bytes 65560
  3.5 0.0 copy-start.3
  3.5 0.7 %copy-done.3 = s32[1,1,8,16]{3,2,1,0:T(8,128)S(1)} copy-done((s32[1,1,8,16]{3,2,1,0:T(8,128)S(1)}, s32[1,1,8,16]{3,2,1,0:T(8,128)}, u32[]{:S(2)}) %copy-start.3) | copy-done | bytes 536
  4.2 0.0 copy-start.4
  4.2 0.7 %copy-done.4 = s32[1,64,4]{1,2,0:T(4,128)S(1)} copy-done((s32[1,64,4]{1,2,0:T(4,128)S(1)}, s32[1,64,4]{1,2,0:T(4,128)}, u32[]{:S(2)}) %copy-start.4) | copy-done | bytes 1048
  4.8 48.4 %shard_map.64 = f32[4,256,128]{2,1,0:T(8,128)S(1)} custom-call(bf16[256,128]{1,0:T(8,128)(2,1)S(1)} %bitcast.10, s32[8,16]{1,0:T(8,128)S(1)} %bitcast.11, s32[4,64]{1,0:T(4,128)S(1)} %bitcast.12, bf16[64,512,128]{2,1,0:T(8,128)(2,1)} %bitcast.13, bf16[64,128,128]{2,1,0:T(8,128)(2,1)S(1)} %copy-done, f32[4,256,128]{2,1,0:T(8,128)S(1)} %bitcast.9), custom_call_target="tpu_custom_call" | custom-call | flops 167772160 | bytes 10485760 | tf_op jit(solution)/shard_map/pallas_call | solution.py:302
  53.2 0.8 %copy.8 = f32[4,64,4,128]{3,2,1,0:T(4,128)} copy(f32[4,64,4,128]{3,2,1,0:T(4,128)S(1)} %bitcast.8) | data formatting | bytes 1048576
Async XLA Ops:
  0.0 1.6 %copy-start = (bf16[64,128,128]{2,1,0:T(8,128)(2,1)S(1)}, bf16[64,128,128]{2,1,0:T(8,128)(2,1)}, u32[]{:S(2)}) copy-start(bf16[64,128,128]{2,1,0:T(8,128)(2,1)} %diag_hbm.1) | copy-start | bytes 6291460
  1.6 1.0 %copy-start.1 = (f32[4,64,4,128]{3,2,1,0:T(4,128)S(1)}, f32[4,64,4,128]{3,2,1,0:T(4,128)}, u32[]{:S(2)}) copy-start(f32[4,64,4,128]{3,2,1,0:T(4,128)} %param.10) | copy-start | bytes 1572868
  2.6 0.8 %copy-start.2 = (bf16[1,64,4,128]{3,2,1,0:T(4,128)(2,1)S(1)}, bf16[1,64,4,128]{3,2,1,0:T(4,128)(2,1)}, u32[]{:S(2)}) copy-start(bf16[1,64,4,128]{3,2,1,0:T(4,128)(2,1)} %param.11) | copy-start | bytes 196612
  3.5 0.7 %copy-start.3 = (s32[1,1,8,16]{3,2,1,0:T(8,128)S(1)}, s32[1,1,8,16]{3,2,1,0:T(8,128)}, u32[]{:S(2)}) copy-start(s32[1,1,8,16]{3,2,1,0:T(8,128)} %param.7) | copy-start | bytes 1540
  4.2 0.7 %copy-start.4 = (s32[1,64,4]{1,2,0:T(4,128)S(1)}, s32[1,64,4]{1,2,0:T(4,128)}, u32[]{:S(2)}) copy-start(s32[1,64,4]{1,2,0:T(4,128)} %param.8) | copy-start | bytes 3076

commit v3 on v2

--- a/solution.py
+++ b/solution.py
@@ -26,12 +26,12 @@
 
 def kernel(
     sizes,
-    history, wanted, slots, tiles_hbm, diag_hbm, excitation_hbm,
+    history_hbm, wanted_hbm, slots_hbm, tiles_hbm, diag_hbm, excitation_hbm,
     out,
-    tiles, diag, excitation, picks, spots, ask_out, ask_in, source, sent, got, lhs,
-    part_own, part_out, part_in, driven,
+    wanted, slots, tiles, diag, excitation, picks, spots, ask_out, ask_in, source, sent, got, lhs,
+    part_out, quarter_in, sum_out, sum_in, driven,
     load_sem, ask_send, ask_recv, shift_send, shift_recv, swap_send, swap_recv,
-    part_send, part_recv, driven_send, driven_recv,
+    part_send, part_recv, sum_send, sum_recv, driven_send, driven_recv,
 ):
     readers, bins, steps, n, listed, exc, cap, width = sizes
     me = lax.axis_index("rows")
@@ -40,14 +40,18 @@
     chunk = cap * exc
     group = 16 // exc
     groups = rows // 16
+    quarter = rows // bins
 
     loads = [
         pltpu.make_async_copy(excitation_hbm, excitation, load_sem.at[0]),
         pltpu.make_async_copy(tiles_hbm, tiles, load_sem.at[1]),
         pltpu.make_async_copy(diag_hbm, diag, load_sem.at[2]),
+        pltpu.make_async_copy(wanted_hbm, wanted, load_sem.at[3]),
+        pltpu.make_async_copy(slots_hbm, slots, load_sem.at[4]),
+        pltpu.make_async_copy(history_hbm, source.at[0], load_sem.at[5]),
     ]
-    for load in loads:
-        load.start()
+    for i in (3, 4, 5, 1, 0, 2):
+        loads[i].start()
 
     barrier = pltpu.get_barrier_semaphore()
     for d in range(1, readers):
@@ -58,6 +62,7 @@
     total = readers * cap
     shape = (total, readers)
     spread = jnp.where(lax.div(row_of(shape), cap) == lane_of(shape), 1.0, 0.0).astype(F32)
+    loads[3].wait()
     every = dot(spread, wanted[...].astype(F32))
     shape = (total, cap)
     own = jnp.where(lax.rem(row_of(shape), cap) == lane_of(shape), every, 0.0)
@@ -88,11 +93,12 @@
 
     def shift(s):
         return pltpu.make_async_remote_copy(
-            src_ref=history, dst_ref=source.at[s],
+            src_ref=source.at[0], dst_ref=source.at[s],
             send_sem=shift_send.at[s], recv_sem=shift_recv.at[s],
             device_id={"delay": lax.rem(bin_at + s, bins)}, device_id_type=MESH,
         )
 
+    loads[5].wait()
     for s in range(1, min(steps, bins)):
         @pl.when(bin_at + s < bins)
         def _():
@@ -100,9 +106,9 @@
 
     mine = pl.ds(pl.multiple_of(me * cap, cap), cap)
     ask_in[mine] = ask_out[mine]
-    source[0] = history[...]
 
     here = lax.div(row_of((rows, n)), exc) == lane_of((rows, n))
+    loads[4].wait()
     listing = slots[...].astype(F32)
     shape = (rows, total * exc)
     lanes = lane_of(shape).astype(F32)
@@ -148,10 +154,30 @@
             device_id={"rows": peer}, device_id_type=MESH,
         )
 
-    def part(t, k):
-        return pltpu.make_async_remote_copy(
-            src_ref=part_out.at[t], dst_ref=part_in.at[t, k],
-            send_sem=part_send.at[t], recv_sem=part_recv.at[t, k],
+    def at_quarter(k):
+        return pl.ds(pl.multiple_of(k * quarter, quarter), quarter)
+
+    def part(t, d):
+        peer = lax.rem(bin_at + d, bins)
+        return pltpu.make_async_remote_copy(
+            src_ref=part_out.at[t, at_quarter(peer)], dst_ref=quarter_in.at[t, bin_at],
+            send_sem=part_send.at[t, d], recv_sem=part_recv.at[t, d],
+            device_id={"delay": peer}, device_id_type=MESH,
+        )
+
+    def parted(t, d):
+        peer = lax.rem(bin_at + bins - d, bins)
+        there = quarter_in.at[t, peer]
+        return pltpu.make_async_remote_copy(
+            src_ref=there, dst_ref=there,
+            send_sem=part_send.at[t, d], recv_sem=part_recv.at[t, d],
+            device_id={"delay": peer}, device_id_type=MESH,
+        )
+
+    def summed(t, k):
+        return pltpu.make_async_remote_copy(
+            src_ref=sum_out.at[t], dst_ref=sum_in.at[t, k],
+            send_sem=sum_send.at[t], recv_sem=sum_recv.at[t, k],
             device_id={"delay": 0}, device_id_type=MESH,
         )
 
@@ -181,7 +207,7 @@
         @pl.when((t > 0) & (bin_at >= t))
         def _():
             pltpu.make_async_remote_copy(
-                src_ref=history, dst_ref=source.at[t],
+                src_ref=source.at[0], dst_ref=source.at[t],
                 send_sem=shift_send.at[t], recv_sem=shift_recv.at[t],
                 device_id={"delay": lax.rem(bin_at + 1, bins)}, device_id_type=MESH,
             ).wait_recv()
@@ -219,23 +245,35 @@
                 at = pl.ds(pl.multiple_of(g * 16, 16), 16)
                 right = jnp.concatenate([tiles[g * group + j] for j in range(group)], axis=1)
                 value = chosen(dot(lhs[at], right))
-                part_out[t, at] = value.astype(BF16)
-                part_own[at] = value
+                part_out[t, at] = value
             return c
 
         lax.fori_loop(0, groups // 4, some, 0)
 
         @pl.when(bin_at > 0)
         def _():
-            part(t, bin_at).start()
+            for d in range(1, bins):
+                part(t, d).start()
+            sum_out[t] = part_out[t, at_quarter(bin_at)]
+            for d in range(1, bins):
+                @pl.when(lax.rem(bin_at + bins - d, bins) > 0)
+                def _():
+                    parted(t, d).wait_recv()
+                    sum_out[t] += quarter_in[t, lax.rem(bin_at + bins - d, bins)]
+            summed(t, bin_at).start()
 
         @pl.when(bin_at == 0)
         def _():
-            value = part_own[...]
+            value = part_out[t, :quarter]
+            for d in range(1, bins):
+                parted(t, d).wait_recv()
+                value = value + quarter_in[t, bins - d]
+            driven[t, :quarter] = (excitation[t, :quarter] - value).astype(BF16)
             for k in range(1, bins):
-                part(t, k).wait_recv()
-                value = value + part_in[t, k].astype(F32)
-            driven[t] = (excitation[t] - value).astype(BF16)
+                here = slice(k * quarter, (k + 1) * quarter)
+                summed(t, k).wait_recv()
+                value = part_out[t, here] + sum_in[t, k]
+                driven[t, here] = (excitation[t, here] - value).astype(BF16)
             for d in range(1, bins):
                 tell(t, d).start()
 
@@ -278,7 +316,9 @@
 
         @pl.when(bin_at > 0)
         def _():
-            part(t, bin_at).wait_send()
+            for d in range(1, bins):
+                part(t, d).wait_send()
+            summed(t, bin_at).wait_send()
 
         @pl.when(bin_at == 0)
         def _():
@@ -301,10 +341,12 @@
     dma = pltpu.SemaphoreType.DMA
     solved = pl.pallas_call(
         functools.partial(kernel, sizes),
-        out_shape=jax.ShapeDtypeStruct((steps, rows, width), F32),
-        in_specs=[vmem, vmem, vmem, anywhere, anywhere, anywhere],
+        out_shape=pltpu.VMEM((steps, rows, width), F32),
+        in_specs=[anywhere] * 6,
         out_specs=vmem,
         scratch_shapes=[
+            pltpu.VMEM((readers, cap), jnp.int32),
+            pltpu.VMEM((listed, n), jnp.int32),
             pltpu.VMEM((n, listed * width, width), BF16),
             pltpu.VMEM((n, width, width), BF16),
             pltpu.VMEM((steps, rows, width), F32),
@@ -316,24 +358,27 @@
             pltpu.VMEM((steps, taken, width), BF16),
             pltpu.VMEM((steps, taken, width), BF16),
             pltpu.VMEM((rows, listed * width), BF16),
-            pltpu.VMEM((rows, width), F32),
+            pltpu.VMEM((steps, rows, width), F32),
+            pltpu.VMEM((steps, bins, rows // bins, width), F32),
+            pltpu.VMEM((steps, rows // bins, width), F32),
+            pltpu.VMEM((steps, bins, rows // bins, width), F32),
             pltpu.VMEM((steps, rows, width), BF16),
-            pltpu.VMEM((steps, bins, rows, width), BF16),
-            pltpu.VMEM((steps, rows, width), BF16),
-            dma((3,)),
+            dma((6,)),
             dma((readers,)),
             dma((readers,)),
             dma((steps,)),
             dma((steps,)),
             dma((steps, readers)),
             dma((steps, readers)),
+            dma((steps, bins)),
+            dma((steps, bins)),
             dma((steps,)),
             dma((steps, bins)),
             dma((steps, bins)),
             dma((steps,)),
         ],
         compiler_params=pltpu.CompilerParams(
-            collective_id=0, has_side_effects=True, vmem_limit_bytes=44 << 20
+            collective_id=0, has_side_effects=True, vmem_limit_bytes=57 << 20
         ),
         cost_estimate=pl.CostEstimate(
             flops=2 * steps * rows * width * width * (listed + 1), transcendentals=0,

time: 54.3 us -> 59.8 us (1.10)
  Pallas kernels: 48.4 us -> 58.9 us
  local copies, waits for them, and re-layouts: 5.63 us -> 0.8 us
    pallas_call x1, Pallas kernels: 48.4 us -> 58.9 us  [body(): pl.pallas_call(functools.partial(kernel, sizes), out_shape=pltpu.VMEM((st...]
    unnamed x11 -> x1, local copies, waits for them, and re-layouts: 5.63 us -> 0.8 us
where the time goes in v3:
time: 59.8 us; the launch traced here: 59.7 us
  Pallas kernels  58.9 us (98%)
  local copies, waits for them, and re-layouts  0.8 us (1%)
    pallas_call x1, Pallas kernels, body(): pl.pallas_call(functools.partial(kernel, sizes), out_shape=pltpu.VMEM((st...  58.9 us

profile of v3, /device:TPU:6, one launch (start us, length us, event | category | flops | bytes accessed | tf_op | source)
XLA Modules:
  0.0 59.7 jit_solution(6677515445240025182)
XLA Ops:
  0.0 58.9 %shard_map.64 = f32[4,256,128]{2,1,0:T(8,128)S(1)} custom-call(bf16[256,128]{1,0:T(8,128)(2,1)} %bitcast.11, s32[8,16]{1,0:T(8,128)} %bitcast.12, s32[4,64]{1,0:T(4,128)} %bitcast.13, bf16[64,512,128]{2,1,0:T(8,128)(2,1)} %bitcast.9, bf16[64,128,128]{2,1,0:T(8,128)(2,1)} %diag_hbm.1, f32[4,256,128]{2,1,0:T(8,128)} %bitcast.10), custom_call_target="tpu_custom_call" | custom-call | flops 167772160 | bytes 10485760 | tf_op jit(solution)/shard_map/pallas_call | solution.py:342
  58.9 0.8 %copy.8 = f32[4,64,4,128]{3,2,1,0:T(4,128)} copy(f32[4,64,4,128]{3,2,1,0:T(4,128)S(1)} %bitcast.8) | data formatting | bytes 1048576

commit v4 on v1

--- a/solution.py
+++ b/solution.py
@@ -26,9 +26,9 @@
 
 def kernel(
     sizes,
-    history, wanted, slots, tiles_hbm, diag_hbm, excitation_hbm,
+    history_hbm, wanted_hbm, slots_hbm, tiles_hbm, diag_hbm, excitation_hbm,
     out,
-    tiles, diag, excitation, picks, spots, ask_out, ask_in, source, sent, got, lhs,
+    wanted, slots, tiles, diag, excitation, picks, spots, ask_out, ask_in, source, sent, got, lhs,
     part_out, part_in, driven,
     load_sem, ask_send, ask_recv, shift_send, shift_recv, swap_send, swap_recv,
     part_send, part_recv, driven_send, driven_recv,
@@ -45,9 +45,12 @@
         pltpu.make_async_copy(excitation_hbm, excitation, load_sem.at[0]),
         pltpu.make_async_copy(tiles_hbm, tiles, load_sem.at[1]),
         pltpu.make_async_copy(diag_hbm, diag, load_sem.at[2]),
+        pltpu.make_async_copy(wanted_hbm, wanted, load_sem.at[3]),
+        pltpu.make_async_copy(slots_hbm, slots, load_sem.at[4]),
+        pltpu.make_async_copy(history_hbm, source.at[0], load_sem.at[5]),
     ]
-    for load in loads:
-        load.start()
+    for i in (3, 4, 5, 1, 0, 2):
+        loads[i].start()
 
     barrier = pltpu.get_barrier_semaphore()
     for d in range(1, readers):
@@ -58,6 +61,7 @@
     total = readers * cap
     shape = (total, readers)
     spread = jnp.where(lax.div(row_of(shape), cap) == lane_of(shape), 1.0, 0.0).astype(F32)
+    loads[3].wait()
     every = dot(spread, wanted[...].astype(F32))
     shape = (total, cap)
     own = jnp.where(lax.rem(row_of(shape), cap) == lane_of(shape), every, 0.0)
@@ -88,11 +92,12 @@
 
     def shift(s):
         return pltpu.make_async_remote_copy(
-            src_ref=history, dst_ref=source.at[s],
+            src_ref=source.at[0], dst_ref=source.at[s],
             send_sem=shift_send.at[s], recv_sem=shift_recv.at[s],
             device_id={"delay": lax.rem(bin_at + s, bins)}, device_id_type=MESH,
         )
 
+    loads[5].wait()
     for s in range(1, min(steps, bins)):
         @pl.when(bin_at + s < bins)
         def _():
@@ -100,9 +105,9 @@
 
     mine = pl.ds(pl.multiple_of(me * cap, cap), cap)
     ask_in[mine] = ask_out[mine]
-    source[0] = history[...]
 
     here = lax.div(row_of((rows, n)), exc) == lane_of((rows, n))
+    loads[4].wait()
     listing = slots[...].astype(F32)
     shape = (rows, total * exc)
     lanes = lane_of(shape).astype(F32)
@@ -163,7 +168,7 @@
         )
 
     def solve(u):
-        later = u + 1 + bin_at
+        later = jnp.minimum(u + 1 + bin_at, steps)
 
         def some(q, c):
             for i in range(4):
@@ -172,39 +177,48 @@
                 right = jnp.concatenate([diag[g * group + j] for j in range(group)], axis=1)
                 value = chosen(dot(driven[u, at], right))
                 out[u, at] = value
-
-                @pl.when(later < steps)
-                def _():
-                    source[jnp.minimum(later, steps - 1), at] = value.astype(BF16)
+                source[later, at] = value.astype(BF16)
             return c
 
         lax.fori_loop(0, groups // 4, some, 0)
 
-    def step(t, carry):
-        @pl.when((t > 0) & (bin_at >= t))
-        def _():
-            pltpu.make_async_remote_copy(
-                src_ref=history, dst_ref=source.at[t],
-                send_sem=shift_send.at[t], recv_sem=shift_recv.at[t],
-                device_id={"delay": lax.rem(bin_at + 1, bins)}, device_id_type=MESH,
-            ).wait_recv()
-
-        @pl.when((bin_at > 0) & (bin_at < t))
-        def _():
-            u = t - 1 - bin_at
-            tell(u, 0).wait_recv()
-
-            @pl.when(u == 0)
-            def _():
-                loads[2].wait()
-
-            solve(u)
-
+    def launch(t):
         sent[t] = dot(picks[...], source[t]).astype(BF16)
         for d in range(1, readers):
             swap(t, d).start()
         mine = pl.ds(pl.multiple_of(me * chunk, chunk), chunk)
         got[t, mine] = sent[t, mine]
+
+    def early(s, c):
+        @pl.when(bin_at >= s)
+        def _():
+            pltpu.make_async_remote_copy(
+                src_ref=source.at[0], dst_ref=source.at[s],
+                send_sem=shift_send.at[s], recv_sem=shift_recv.at[s],
+                device_id={"delay": lax.rem(bin_at + 1, bins)}, device_id_type=MESH,
+            ).wait_recv()
+            launch(s)
+        return c
+
+    launch(0)
+    lax.fori_loop(1, steps, early, 0)
+
+    def step(t, carry):
+        @pl.when((bin_at > 0) & (bin_at < t))
+        def _():
+            u = t - 1 - bin_at
+            tell(u, 0).wait_recv()
+
+            @pl.when(u == 0)
+            def _():
+                loads[2].wait()
+
+            solve(u)
+
+        @pl.when(bin_at < t)
+        def _():
+            launch(t)
+
         for d in range(1, readers):
             swapped(t, d).wait_recv()
         arrived = got[t]
@@ -221,7 +235,8 @@
                 g = q * 4 + i
                 at = pl.ds(pl.multiple_of(g * 16, 16), 16)
                 right = jnp.concatenate([tiles[g * group + j] for j in range(group)], axis=1)
-                part_out[t, at] = chosen(dot(lhs[at], right))
+                value = chosen(dot(lhs[at], right))
+                part_out[t, at] = value
             return c
 
         lax.fori_loop(0, groups // 4, some, 0)
@@ -298,14 +313,16 @@
     rows, taken = n * exc, readers * cap * exc
     sizes = (readers, bins, steps, n, listed, exc, cap, width)
     vmem = pl.BlockSpec(memory_space=pltpu.VMEM)
-    anywhere = pl.BlockSpec(memory_space=pl.ANY)
+    anywhere = pl.BlockSpec(memory_space=pltpu.HBM)
     dma = pltpu.SemaphoreType.DMA
     solved = pl.pallas_call(
         functools.partial(kernel, sizes),
-        out_shape=jax.ShapeDtypeStruct((steps, rows, width), F32),
-        in_specs=[vmem, vmem, vmem, anywhere, anywhere, anywhere],
+        out_shape=pltpu.VMEM((steps, rows, width), F32),
+        in_specs=[anywhere] * 6,
         out_specs=vmem,
         scratch_shapes=[
+            pltpu.VMEM((readers, cap), jnp.int32),
+            pltpu.VMEM((listed, n), jnp.int32),
             pltpu.VMEM((n, listed * width, width), BF16),
             pltpu.VMEM((n, width, width), BF16),
             pltpu.VMEM((steps, rows, width), F32),
@@ -313,14 +330,14 @@
             pltpu.VMEM((listed, rows, taken), BF16),
             pltpu.VMEM((readers * cap, width), F32),
             pltpu.VMEM((readers * cap, width), F32),
-            pltpu.VMEM((steps, rows, width), BF16),
+            pltpu.VMEM((steps + 1, rows, width), BF16),
             pltpu.VMEM((steps, taken, width), BF16),
             pltpu.VMEM((steps, taken, width), BF16),
             pltpu.VMEM((rows, listed * width), BF16),
             pltpu.VMEM((steps, rows, width), F32),
             pltpu.VMEM((steps, bins, rows, width), F32),
             pltpu.VMEM((steps, rows, width), BF16),
-            dma((3,)),
+            dma((6,)),
             dma((readers,)),
             dma((readers,)),
             dma((steps,)),

time: 60.3 us -> 60.9 us (level)
  Pallas kernels: 58.2 us -> 60 us
  local copies, waits for them, and re-layouts: 1.87 us -> 0.8 us
    pallas_call x1, Pallas kernels: 58.2 us -> 60 us  [body(): pl.pallas_call(functools.partial(kernel, sizes), out_shape=pltpu.VMEM((st...]
    unnamed x1, local copies, waits for them, and re-layouts: 1.87 us -> 0.8 us
where the time goes in v4:
time: 60.9 us; the launch traced here: 60.8 us
  Pallas kernels  60 us (99%)
  local copies, waits for them, and re-layouts  0.8 us (1%)
    pallas_call x1, Pallas kernels, body(): pl.pallas_call(functools.partial(kernel, sizes), out_shape=pltpu.VMEM((st...  60 us

profile of v4, /device:TPU:6, one launch (start us, length us, event | category | flops | bytes accessed | tf_op | source)
XLA Modules:
  0.0 60.8 jit_solution(9626788323153027296)
XLA Ops:
  0.0 60.0 %shard_map.64 = f32[4,256,128]{2,1,0:T(8,128)S(1)} custom-call(bf16[256,128]{1,0:T(8,128)(2,1)} %bitcast.11, s32[8,16]{1,0:T(8,128)} %bitcast.12, s32[4,64]{1,0:T(4,128)} %bitcast.13, bf16[64,512,128]{2,1,0:T(8,128)(2,1)} %bitcast.9, bf16[64,128,128]{2,1,0:T(8,128)(2,1)} %diag_hbm.1, f32[4,256,128]{2,1,0:T(8,128)} %bitcast.10), custom_call_target="tpu_custom_call" | custom-call | flops 167772160 | bytes 10485760 | tf_op jit(solution)/shard_map/pallas_call | solution.py:318
  60.0 0.8 %copy.8 = f32[4,64,4,128]{3,2,1,0:T(4,128)} copy(f32[4,64,4,128]{3,2,1,0:T(4,128)S(1)} %bitcast.8) | data formatting | bytes 1048576

commit v5 on v4

--- a/solution.py
+++ b/solution.py
@@ -157,7 +157,7 @@
         return pltpu.make_async_remote_copy(
             src_ref=part_out.at[t], dst_ref=part_in.at[t, k],
             send_sem=part_send.at[t], recv_sem=part_recv.at[t, k],
-            device_id={"delay": 0}, device_id_type=MESH,
+            device_id={"delay": jnp.where(bin_at == 1, 0, lax.rem(bin_at, 2))}, device_id_type=MESH,
         )
 
     def tell(t, d):
@@ -241,6 +241,12 @@
 
         lax.fori_loop(0, groups // 4, some, 0)
 
+        @pl.when(bin_at == 1)
+        def _():
+            for k in range(3, bins, 2):
+                part(t, k).wait_recv()
+                part_out[t] += part_in[t, k]
+
         @pl.when(bin_at > 0)
         def _():
             part(t, bin_at).start()
@@ -248,7 +254,7 @@
         @pl.when(bin_at == 0)
         def _():
             value = part_out[t]
-            for k in range(1, bins):
+            for k in [*range(2, bins, 2), 1]:
                 part(t, k).wait_recv()
                 value = value + part_in[t, k]
             driven[t] = (excitation[t] - value).astype(BF16)

time: 60.9 us -> 54.5 us (0.89)
  Pallas kernels: 60 us -> 53.5 us
    pallas_call x1, Pallas kernels: 60 us -> 53.5 us  [body(): pl.pallas_call(functools.partial(kernel, sizes), out_shape=pltpu.VMEM((st...]
where the time goes in v5:
time: 54.5 us; the launch traced here: 54.3 us
  Pallas kernels  53.5 us (98%)
  local copies, waits for them, and re-layouts  0.8 us (1%)
    pallas_call x1, Pallas kernels, body(): pl.pallas_call(functools.partial(kernel, sizes), out_shape=pltpu.VMEM((st...  53.5 us

profile of v5, /device:TPU:6, one launch (start us, length us, event | category | flops | bytes accessed | tf_op | source)
XLA Modules:
  0.0 54.3 jit_solution(9501445339367990423)
XLA Ops:
  0.0 53.5 %shard_map.64 = f32[4,256,128]{2,1,0:T(8,128)S(1)} custom-call(bf16[256,128]{1,0:T(8,128)(2,1)} %bitcast.11, s32[8,16]{1,0:T(8,128)} %bitcast.12, s32[4,64]{1,0:T(4,128)} %bitcast.13, bf16[64,512,128]{2,1,0:T(8,128)(2,1)} %bitcast.9, bf16[64,128,128]{2,1,0:T(8,128)(2,1)} %diag_hbm.1, f32[4,256,128]{2,1,0:T(8,128)} %bitcast.10), custom_call_target="tpu_custom_call" | custom-call | flops 167772160 | bytes 10485760 | tf_op jit(solution)/shard_map/pallas_call | solution.py:324
  53.5 0.8 %copy.8 = f32[4,64,4,128]{3,2,1,0:T(4,128)} copy(f32[4,64,4,128]{3,2,1,0:T(4,128)S(1)} %bitcast.8) | data formatting | bytes 1048576
